TPU v7x, 256 devices: a whole 4x4x8 slice. The times are simulated.
256 devices in a mesh: region: 16 (over z, x_lo), neuron: 16 (over x_hi, y, core).
Axes of the slice: x: 4 (x_hi: 2, x_lo: 2; x = x_hi * 2 + x_lo), y: 4, z: 8, core: 2. Of those that a mesh axis runs over, the one named last changes fastest.
Arguments:
- counts: bfloat16 [16, 20480, 4096], P('region', 'neuron'), may hold values from 0 to 3, as said below
- latents: bfloat16 [64, 4096], P(None, 'neuron'), may hold values from -5 to 5
- loadings: bfloat16 [16, 64, 20480], P('region', None, 'neuron'), may hold values from -0.75 to 0.75
- bias: float32 [16, 20480], P('region', 'neuron'), may hold values from -3 to 3
- delays: int32 [16, 64], P('region'), may hold values from 0 to 128
- recorded: int32 [16], P('region'), may hold values from 1024 to 4096, as said below
Outputs:
- grad_latents: float32 [64, 4096], P(None, 'neuron')
- grad_loadings: float32 [16, 64, 20480], P('region', None, 'neuron')
- grad_bias: float32 [16, 20480], P('region', 'neuron')
Inputs may be any that keep to these rules, and one draw needn't show every extreme that they name: At least one region is recorded over all 4096 bins. `counts`: whole numbers.
All inputs are finite; a program needn't handle non-finite values.
Results may differ from a plain program's by a relative error of at most 0.0021.
Values may be sent and summed in bfloat16 or wider, within the bound.
A program may use at most 64 MiB of HBM per device.

v0:
```python
import jax
import jax.numpy as jnp
from jax import lax
from jax.sharding import PartitionSpec as P


def move_rows(source, delay_row, levels, forward):
    current = source
    for level in range(levels):
        amount = 1 << level
        if forward:
            displaced = jnp.pad(current[:, :-amount], ((0, 0), (amount, 0)))
        else:
            displaced = jnp.pad(current[:, amount:], ((0, 0), (0, amount)))
        chosen = delay_row // amount % 2 == 1
        current = jnp.where(chosen[:, None], displaced, current)
    return current


def delay_rows(source, delay_row, offset, span):
    result = move_rows(source, delay_row, offset.bit_length(), True)
    return result[:, offset : offset + span]


def advance_rows(source, delay_row, span, largest):
    result = move_rows(source, delay_row, largest.bit_length(), False)
    return result[:, :span]


def per_device(counts, latents, loadings, bias, delays, recorded):
    count_rows = counts[0]
    load = loadings[0]
    bias_row = bias[0]
    delay_row = delays[0]
    length = recorded[0]
    width = latents.shape[1]
    total = count_rows.shape[1]
    reach = width // 2
    lat_count = latents.shape[0]
    neu_count = count_rows.shape[0]

    def accumulate(carry, piece, start):
        grad_load, grad_bias, grad_shift = carry
        span = piece.shape[1]
        observed = lax.dynamic_slice_in_dim(count_rows, start, span, 1).astype(jnp.float32)
        eta = lax.dot_general(
            load, piece, (((0,), (0,)), ((), ())), preferred_element_type=jnp.float32
        )
        eta = eta + bias_row[:, None]
        bins = start + jnp.arange(span, dtype=jnp.int32)
        resid = jnp.where((bins < length)[None, :], jnp.exp(eta) - observed, 0.0)
        resid_low = resid.astype(jnp.bfloat16)
        grad_load = grad_load + lax.dot_general(
            piece, resid_low, (((1,), (1,)), ((), ())), preferred_element_type=jnp.float32
        )
        grad_bias = grad_bias + jnp.sum(resid, axis=1)
        block = jnp.dot(load, resid_low, preferred_element_type=jnp.float32)
        grad_shift = lax.dynamic_update_slice_in_dim(grad_shift, block, start, 1)
        return (grad_load, grad_bias, grad_shift)

    initial = (
        jnp.zeros((lat_count, neu_count), jnp.float32),
        jnp.zeros((neu_count,), jnp.float32),
        jnp.zeros((lat_count, total), jnp.float32),
    )
    whole = lax.all_gather(latents, "neuron", axis=1, tiled=True)
    shifted = delay_rows(jnp.pad(whole, ((0, 0), (reach, 0))), delay_row, reach, total)

    def visit(step, carry):
        begin = (step * width).astype(jnp.int32)
        return accumulate(carry, lax.dynamic_slice_in_dim(shifted, begin, width, 1), begin)

    grad_load, grad_bias, grad_shift = lax.fori_loop(0, total // width, visit, initial)
    source = advance_rows(jnp.pad(grad_shift, ((0, 0), (0, reach))), delay_row, total, reach)
    summed = lax.psum_scatter(source, "neuron", scatter_dimension=1, tiled=True)
    grad_latents = lax.psum(summed, "region")
    return (grad_latents, grad_load[None], grad_bias[None])


def solution(mesh):
    placed = (
        P("region", "neuron", None),
        P(None, "neuron"),
        P("region", None, "neuron"),
        P("region", "neuron"),
        P("region", None),
        P("region"),
    )
    return jax.shard_map(
        per_device,
        mesh=mesh,
        in_specs=placed,
        out_specs=(P(None, "neuron"), P("region", None, "neuron"), P("region", "neuron")),
        check_vma=False,
    )
```

profile of v0, /device:TPU:2, one launch (start us, length us, event | category | flops | bytes accessed | tf_op | source)
XLA Modules:
  0.0 316.0 jit_solution(13940699881098271327)
XLA Ops:
  7.9 25.2 %all_gather.3 = bf16[64,4096]{1,0:T(8,128)(2,1)S(1)} all-gather(bf16[64,256]{1,0:T(8,128)(2,1)} %param.9), channel_id=1, replica_groups=mesh['region'=16,'neuron'=16] {'neuron'}, dimensions={1}, use_global_device_ids=true | all-gather | bytes 557056 | tf_op jit(solution)/shard_map/all_gather | solution.py:66
  35.1 14.5 %copy.9 = bf16[1,1280,4096]{1,2,0:T(8,128)(2,1)} copy(bf16[1,1280,4096]{2,1,0:T(8,128)(2,1)} %param.8) | data formatting | bytes 20971520 | tf_op args[0]
  49.8 0.7 copy-done.1
  50.5 47.3 %while.18 = (s32[]{:T(128)}, f32[64,1280]{1,0:T(8,128)S(1)}, f32[1280]{0:T(1024)S(1)}, f32[64,4096]{1,0:T(8,128)S(1)}, bf16[64,4096]{1,0:T(8,128)(2,1)S(1)}, /*i...) while((s32[]{:T(128)}, f32[64,1280]{1,0:T(8,128)S(1)}, ...), condition=%wide.region_2.3_spmd.clone, body=%wide.region_0.2_spmd.clone.sunk | while | flops 127960832 | bytes 3776474 | solution.py:73
  51.2 1.6 fusion.44
  54.1 1.6 fusion.44
  57.1 1.6 fusion.44
  60.1 1.6 fusion.44
  63.0 1.6 fusion.44
  66.0 1.6 fusion.44
  68.9 1.6 fusion.44
  71.9 1.6 fusion.44
  74.8 1.6 fusion.44
  77.8 1.6 fusion.44
  80.8 1.6 fusion.44
  83.7 1.6 fusion.44
  86.7 1.6 fusion.44
  89.6 1.6 fusion.44
  92.6 1.6 fusion.44
  95.6 1.6 fusion.44
  101.8 1.2 slice_select_fusion
  103.0 73.4 %reduce-scatter.2.cloned.1.call-done = f32[64,256]{1,0:T(8,128)} async-done(((f32[64,4096]{1,0:T(8,128)}), f32[64,256]{1,0:T(8,128)}) %reduce-scatter.2.cloned.1.call-update) | async-done | bytes 65552 | tf_op jit(solution)/shard_map/reduce_scatter | solution.py:75
  177.0 130.6 %all-reduce.20.cloned.1.call-done = f32[64,256]{1,0:T(8,128)} async-done(((f32[64,256]{1,0:T(8,128)}), f32[64,256]{1,0:T(8,128)}) %all-reduce.20.cloned.1.call-update) | async-done | bytes 65552 | tf_op jit(solution)/shard_map/psum | solution.py:76
  307.7 1.5 copy.24
  (119 shorter events, 27.9 us)
Async XLA Ops:
  7.2 169.2 %reduce-scatter.2.cloned.1.call-start = ((), (), s32[]{:S(2)}) async-start(), calls=%async_computation.1 | async-start | bytes 1114112 | tf_op jit(solution)/shard_map/reduce_scatter | solution.py:75
  49.6 0.9 copy-start.1
  49.6 0.9 copy-start.2
  97.8 0.8 copy-start
  103.0 204.7 %all-reduce.20.cloned.1.call-start = ((), (), s32[]{:S(2)}) async-start(), calls=%async_computation.2 | async-start | bytes 131072 | tf_op jit(solution)/shard_map/psum | solution.py:76
Sparse Core Ops, SparseCore 0:
  103.1 73.2 reduce-scatter.1
  179.2 128.4 all-reduce.19
where the time goes:
time: 318 us; the launch traced here: 316 us
  waiting for transfers between devices  204 us (64%)
  matrix products  35.2 us (11%)
  blocking collectives  25.2 us (8%)
  local copies, waits for them, and re-layouts  20.1 us (6%)
  other arithmetic  16.5 us (5%)
  between operations  14.2 us (4%)
    psum x1, waiting for transfers between devices, per_device(): grad_latents = lax.psum(summed, 'region')  131 us
    reduce_scatter x1, waiting for transfers between devices, per_device(): summed = lax.psum_scatter(source, 'neuron', scatter_dimension=1, tiled=True)  73.4 us
    dot_general x16, matrix products, accumulate(): lax.dot_general(load, piece, (((0,), (0,)), ((), ())), preferred_element_...  26.2 us
    all_gather x1, blocking collectives, per_device(): whole = lax.all_gather(latents, 'neuron', axis=1, tiled=True)  25.2 us
    unnamed x8, local copies, waits for them, and re-layouts  16.9 us
    lt x16, other arithmetic, accumulate(): resid = jnp.where((bins < length)[None, :], jnp.exp(eta) - observed, 0.0)  10.9 us
  transfers between devices with their start and end apart: 2, of which 2 were waited for; matrix products, arithmetic and copies ran while one was open for 0% of the time, Pallas kernels for 0%

commit v1 on v0

v1 whole, which is shorter than its diff:
```python
import functools

import jax
import jax.numpy as jnp
from jax import lax
from jax.experimental import pallas as pl
from jax.experimental.pallas import tpu as pltpu
from jax.sharding import PartitionSpec as P

MESH = pl.DeviceIdType.MESH
LANES = 128
LAT = 64
NEU = 1280
TIME = 4096
TILES = TIME // LANES
CHIPS = 8
CHUNK = CHIPS * LANES
DEPTH = 128
ROWS = 4
F32 = jnp.float32
BF16 = jnp.bfloat16


def split_three(value):
    high = value.astype(BF16)
    rest = value - high.astype(F32)
    middle = rest.astype(BF16)
    return high.astype(F32), middle.astype(F32), rest - middle.astype(F32)


def kernel(
    counts_hbm, lat_ref, load_ref, bias_ref, delay_ref, rec_ref,
    out_lat, out_load, out_bias,
    counts, latb, rot, piece, load_t, bias_sum, spun, part, mate_in, pair, plane_in, mine, final_in,
    cnt_sem, ag_send, ag_recv, fw_send, fw_recv, a_send, a_recv, b_send, b_recv, c_send, c_recv,
):
    region = lax.axis_index("region")
    neuron = lax.axis_index("neuron")
    z, x_lo = region // 2, region % 2
    x_hi, y, core = neuron // 8, (neuron // 2) % 4, neuron % 2
    chip = neuron // 2
    x = x_hi * 2 + x_lo
    mate = (region, chip * 2 + 1 - core)

    block = NEU // ROWS
    loads = []
    for k in range(ROWS):
        rows = pl.ds(k * block, block)
        copy = pltpu.make_async_copy(counts_hbm.at[rows], counts.at[rows], cnt_sem.at[k])
        copy.start()
        loads.append(copy)

    plane = []
    for dx in range(4):
        for dy in range(4):
            if (dx, dy) != (0, 0):
                px, py = (x + dx) % 4, (y + dy) % 4
                plane.append(((z * 2 + px % 2), (px // 2) * 4 + py, px % 2))
    spread = []
    for dz in (0, 1, 7, 2, 6, 3, 5, 4):
        for dl in range(2):
            if (dz, dl) != (0, 0):
                spread.append((((z + dz) % 8), (x_lo + dl) % 2))

    barrier = pltpu.get_barrier_semaphore()
    pl.semaphore_signal(barrier, inc=1, device_id=mate, device_id_type=MESH)
    for reg, pos, _ in plane:
        pl.semaphore_signal(barrier, inc=1, device_id=(reg, pos * 2 + core), device_id_type=MESH)
    for pz, pl_lo in spread[1:]:
        pl.semaphore_signal(barrier, inc=1, device_id=(pz * 2 + pl_lo, neuron), device_id_type=MESH)
    pl.semaphore_wait(barrier, 1 + len(plane) + len(spread) - 1)

    sends = []

    def to_mate(source, pos):
        copy = pltpu.make_async_remote_copy(
            src_ref=source, dst_ref=latb.at[core, pos], send_sem=fw_send.at[pos], recv_sem=fw_recv.at[pos],
            device_id=mate, device_id_type=MESH,
        )
        copy.start()
        return copy

    arrivals = []
    for dxh, dy in ((0, 1), (0, 3), (1, 0), (0, 2), (1, 1), (1, 3), (1, 2)):
        px = 3 - x if dxh else x
        pos = (px // 2) * 4 + (y + dy) % 4
        copy = pltpu.make_async_remote_copy(
            src_ref=lat_ref, dst_ref=latb.at[core, chip], send_sem=ag_send.at[pos], recv_sem=ag_recv.at[chip],
            device_id=(z * 2 + px % 2, pos * 2 + core), device_id_type=MESH,
        )
        copy.start()
        sends.append(copy)
        arrivals.append(pos)
    sends.append(to_mate(lat_ref, chip))
    latb[core, chip] = lat_ref[...]

    ba, bb, bc = split_three(bias_ref[...])
    stacked = jnp.concatenate([load_ref[...].astype(F32), ba, bb, bc, jnp.zeros((DEPTH - LAT - 3, NEU), F32)], axis=0)
    load_t[...] = jnp.transpose(stacked).astype(BF16)
    tail = lax.broadcasted_iota(jnp.int32, (DEPTH - LAT, CHUNK), 0)
    piece[LAT:] = jnp.where(tail < 3, 1.0, 0.0).astype(BF16)
    out_load[...] = jnp.zeros_like(out_load)
    bias_sum[...] = jnp.zeros_like(bias_sum)
    rot[0] = jnp.zeros((LAT, LANES), F32)
    spun[TILES] = jnp.zeros((LAT, LANES), F32)
    same = lax.broadcasted_iota(jnp.int32, (LAT, LAT), 0) == lax.broadcasted_iota(jnp.int32, (LAT, LAT), 1)
    delay = jnp.sum(jnp.where(same, delay_ref[...].astype(F32), 0.0), axis=1, keepdims=True).astype(jnp.int32)
    lane = lax.broadcasted_iota(jnp.int32, (LAT, LANES), 1)
    back = (lane - delay) & (LANES - 1)
    ahead = (lane + delay) & (LANES - 1)
    kept = lane >= delay
    near = lane + delay < LANES
    recorded = rec_ref[0]

    for pos in arrivals:
        pltpu.make_async_copy(lat_ref, latb.at[core, pos], ag_recv.at[pos]).wait()
        sends.append(to_mate(latb.at[core, pos], pos))
    for pos in [chip] + arrivals:
        pltpu.make_async_copy(lat_ref, latb.at[1 - core, pos], fw_recv.at[pos]).wait()

    for tile in range(TILES):
        source = latb[(tile // 2) % 2, tile // 4, :, (tile % 2) * LANES : (tile % 2 + 1) * LANES]
        rot[tile + 1] = jnp.take_along_axis(source.astype(F32), back, axis=1)
    for copy in loads:
        copy.wait()

    def reduce_cores(group):
        def fill(pos, carry):
            for owner in range(2):
                kind = (0, 3)[owner] if group == 0 else (1, 2)[owner]
                tile = pos * 4 + kind
                part[group, owner, pos] = jnp.where(near, spun[tile], spun[tile + 1])
            return carry

        lax.fori_loop(0, CHIPS, fill, 0)
        copy = pltpu.make_async_remote_copy(
            src_ref=part.at[group, 1 - core], dst_ref=mate_in.at[group], send_sem=a_send.at[group],
            recv_sem=a_recv.at[group], device_id=mate, device_id_type=MESH,
        )
        copy.start()
        return copy

    def reduce_plane(group, waiting):
        waiting.wait_recv()
        for pos in range(CHIPS):
            total = part[group, core, pos] + mate_in[group, pos]
            pair[group, 2 * pos] = total[: LAT // 2]
            pair[group, 2 * pos + 1] = total[LAT // 2 :]
        me = chip * 2 + x_lo
        copies = []
        for k, (reg, pos, lo) in enumerate(plane):
            copy = pltpu.make_async_remote_copy(
                src_ref=pair.at[group, pos * 2 + lo], dst_ref=plane_in.at[group, me], send_sem=b_send.at[group, k],
                recv_sem=b_recv.at[group, me], device_id=(reg, pos * 2 + core), device_id_type=MESH,
            )
            copy.start()
            copies.append(copy)
        plane_in[group, me] = pair[group, me]
        return copies

    def reduce_region(group):
        for _, pos, lo in plane:
            pltpu.make_async_copy(pair.at[group, 0], plane_in.at[group, pos * 2 + lo], b_recv.at[group, pos * 2 + lo]).wait()
        total = plane_in[group, 0]
        for k in range(1, 2 * CHIPS):
            total = total + plane_in[group, k]
        mine[group] = total
        copies = []
        for k, (pz, lo) in enumerate(spread):
            copy = pltpu.make_async_remote_copy(
                src_ref=mine.at[group], dst_ref=final_in.at[group, region], send_sem=c_send.at[group, k],
                recv_sem=c_recv.at[group, region], device_id=(pz * 2 + lo, neuron), device_id_type=MESH,
            )
            copy.start()
            copies.append(copy)
        final_in[group, region] = total
        return copies

    def finish(group):
        for pz, lo in spread:
            pltpu.make_async_copy(mine.at[group], final_in.at[group, pz * 2 + lo], c_recv.at[group, pz * 2 + lo]).wait()
        start = pl.multiple_of((core if group == 0 else 1 - core) * LANES, LANES)
        for lo in range(2):
            total = final_in[group, lo]
            for k in range(1, 8):
                total = total + final_in[group, 2 * k + lo]
            out_lat[lo * (LAT // 2) : (lo + 1) * (LAT // 2), pl.ds(start, LANES)] = total

    def chunk(step, carry):
        kind = (5 - step) % 4
        for pos in range(CHIPS):
            tile = pos * 4 + kind
            piece[:LAT, pos * LANES : (pos + 1) * LANES] = jnp.where(kept, rot[tile + 1], rot[tile]).astype(BF16)
        bins = lax.broadcasted_iota(jnp.int32, (1, CHUNK), 1)
        bins = (bins // LANES) * (4 * LANES) + kind * LANES + bins % LANES
        eta = jnp.dot(load_t[...], piece[...], preferred_element_type=F32)
        observed = jnp.concatenate(
            [counts[:, pl.ds(pl.multiple_of((pos * 4 + kind) * LANES, LANES), LANES)] for pos in range(CHIPS)], axis=1
        )
        resid = jnp.where(bins < recorded, jnp.exp(eta) - observed.astype(F32), 0.0)
        total = resid[:, :LANES]
        for pos in range(1, CHIPS):
            total = total + resid[:, pos * LANES : (pos + 1) * LANES]
        bias_sum[...] += total
        low = resid.astype(BF16)
        out_load[...] += lax.dot_general(piece[:LAT], low, (((1,), (1,)), ((), ())), preferred_element_type=F32)
        shift = jnp.dot(load_ref[...], low, preferred_element_type=F32)
        for pos in range(CHIPS):
            spun[pos * 4 + kind] = jnp.take_along_axis(shift[:, pos * LANES : (pos + 1) * LANES], ahead, axis=1)
        return carry

    lax.fori_loop(0, 3, chunk, 0)
    first = reduce_cores(0)
    lax.fori_loop(3, 4, chunk, 0)
    second = reduce_cores(1)
    sends += [first, second]
    sends += reduce_plane(0, first)
    sends += reduce_plane(1, second)
    out_bias[...] = jnp.sum(jnp.transpose(bias_sum[...]), axis=0, keepdims=True)
    sends += reduce_region(0)
    sends += reduce_region(1)
    finish(0)
    finish(1)
    for copy in sends:
        copy.wait_send()


def per_device(counts, latents, loadings, bias, delays, recorded):
    vmem = pl.BlockSpec(memory_space=pltpu.VMEM)
    half = (LAT // 2, LANES)
    grad_lat, grad_load, grad_bias = pl.pallas_call(
        kernel,
        out_shape=(
            jax.ShapeDtypeStruct((LAT, 2 * LANES), F32),
            jax.ShapeDtypeStruct((LAT, NEU), F32),
            jax.ShapeDtypeStruct((1, NEU), F32),
        ),
        in_specs=[pl.BlockSpec(memory_space=pl.ANY), vmem, vmem, vmem, vmem, pl.BlockSpec(memory_space=pltpu.SMEM)],
        out_specs=(vmem, vmem, vmem),
        scratch_shapes=[
            pltpu.VMEM((NEU, TIME), BF16),
            pltpu.VMEM((2, CHIPS, LAT, 2 * LANES), BF16),
            pltpu.VMEM((TILES + 1, LAT, LANES), F32),
            pltpu.VMEM((DEPTH, CHUNK), BF16),
            pltpu.VMEM((NEU, DEPTH), BF16),
            pltpu.VMEM((NEU, LANES), F32),
            pltpu.VMEM((TILES + 1, LAT, LANES), F32),
            pltpu.VMEM((2, 2, CHIPS, LAT, LANES), F32),
            pltpu.VMEM((2, CHIPS, LAT, LANES), F32),
            pltpu.VMEM((2, 2 * CHIPS) + half, F32),
            pltpu.VMEM((2, 2 * CHIPS) + half, F32),
            pltpu.VMEM((2,) + half, F32),
            pltpu.VMEM((2, 16) + half, F32),
            pltpu.SemaphoreType.DMA((ROWS,)),
            pltpu.SemaphoreType.DMA((CHIPS,)),
            pltpu.SemaphoreType.DMA((CHIPS,)),
            pltpu.SemaphoreType.DMA((CHIPS,)),
            pltpu.SemaphoreType.DMA((CHIPS,)),
            pltpu.SemaphoreType.DMA((2,)),
            pltpu.SemaphoreType.DMA((2,)),
            pltpu.SemaphoreType.DMA((2, 15)),
            pltpu.SemaphoreType.DMA((2, 16)),
            pltpu.SemaphoreType.DMA((2, 15)),
            pltpu.SemaphoreType.DMA((2, 16)),
        ],
        compiler_params=pltpu.CompilerParams(
            collective_id=0, has_side_effects=True, vmem_limit_bytes=58 * 2**20
        ),
    )(counts[0], latents, loadings[0], bias, delays, recorded)
    return grad_lat, grad_load[None], grad_bias


def solution(mesh):
    placed = (
        P("region", "neuron", None),
        P(None, "neuron"),
        P("region", None, "neuron"),
        P("region", "neuron"),
        P("region", None),
        P("region"),
    )
    return jax.shard_map(
        per_device,
        mesh=mesh,
        in_specs=placed,
        out_specs=(P(None, "neuron"), P("region", None, "neuron"), P("region", "neuron")),
        check_vma=False,
    )
```

time: 318 us -> 57.8 us (0.18)
  the two profiles are of different devices: /device:TPU:2 before, /device:TPU:1 now
where the time goes in v1:
time: 57.8 us; the launch traced here: 57.5 us
  Pallas kernels  51.8 us (90%)
  local copies, waits for them, and re-layouts  4.47 us (8%)
  between operations  1.29 us (2%)
    pallas_call x1, Pallas kernels, per_device(): pl.pallas_call(kernel, out_shape=(jax.ShapeDtypeStruct((LAT, 2 * LANES),...  51.8 us
    unnamed x3, local copies, waits for them, and re-layouts  4.47 us

profile of v1, /device:TPU:1, one launch (start us, length us, event | category | flops | bytes accessed | tf_op | source)
XLA Modules:
  0.0 57.5 jit_solution(15351805490362676810)
XLA Ops:
  1.3 51.8 %shard_map.85 = (f32[64,256]{1,0:T(8,128)}, f32[64,1280]{1,0:T(8,128)}, f32[1,1280]{1,0:T(1,128)}) custom-call(bf16[1280,4096]{1,0:T(8,128)(2,1)} %bitcast.3, bf16[64,256]{1,0:T(8,128)(2,1)} %lat_ref.1, bf16[64,1280]{1,0:T(8,128)(2,1)} %bitcast.5, f32[1,1280]{1,0:T(1,128)} %bias_ref.1, s32[1,64]{1,0:T(1,128)} %delay_ref.1, s32[1]{0:T(128)S(6)} %copy.12.rec_ref), custom_call_target="tpu_custom_call" | custom-call | tf_op jit(solution)/shard_map/pallas_call | solution.py:231
  53.1 1.5 %copy.13 = f32[64,256]{1,0:T(8,128)} copy(f32[64,256]{1,0:T(8,128)} %get-tuple-element.12) | data formatting | bytes 131072
  54.5 1.7 %copy.14 = f32[1,64,1280]{2,1,0:T(8,128)} copy(f32[1,64,1280]{2,1,0:T(8,128)} %bitcast.4) | data formatting | bytes 655360
  56.3 1.3 %copy.15 = f32[1,1280]{1,0:T(1,128)} copy(f32[1,1280]{1,0:T(1,128)} %get-tuple-element.14) | data formatting | bytes 10240

commit v2 on v0

v2 whole, which is shorter than its diff:
```python
import functools

import jax
import jax.numpy as jnp
from jax import lax
from jax.experimental import pallas as pl
from jax.experimental.pallas import tpu as pltpu
from jax.sharding import PartitionSpec as P

MESH = pl.DeviceIdType.MESH
LANES = 128
LAT = 64
HALF = LAT // 2
NEU = 1280
TIME = 4096
TILES = TIME // LANES
CHIPS = 8
CHUNK = CHIPS * LANES
DEPTH = 128
ROWS = 4
BLOCK = 256
CODED = LAT + 16
BITS = 14
NEAR = ((0, 1), (0, 3), (1, 0), (0, 2), (1, 1), (1, 3), (1, 2))
F32 = jnp.float32
BF16 = jnp.bfloat16
I16 = jnp.int16


def split_three(value):
    high = value.astype(BF16)
    rest = value - high.astype(F32)
    middle = rest.astype(BF16)
    return high.astype(F32), middle.astype(F32), rest - middle.astype(F32)


def exponent_of(largest):
    return jnp.floor(jnp.log2(jnp.maximum(largest, 1e-30))) + 1.0


def encode(value, exponent):
    return jnp.round(value * jnp.exp2(BITS - exponent)).astype(jnp.int32).astype(I16)


def stamp(exponent):
    return jnp.broadcast_to(exponent, (CODED - LAT, LANES)).astype(jnp.int32).astype(I16)


def decode(ref, *index):
    whole = ref[index].astype(jnp.int32).astype(F32)
    return whole[:LAT] * jnp.exp2(whole[LAT : LAT + 1] - BITS)


def kernel(
    counts_hbm, lat_hbm, load_hbm, bias_hbm, delay_hbm, rec_ref,
    out_lat, out_load, out_bias,
    counts, load_ref, bias_ref, delay_ref, latb, rot, piece, load_t, bias_sum, spun, part, mate_in, pair, plane_in,
    mine, final_in, grad_lat, grad_load, grad_bias,
    in_sem, cnt_sem, ag_send, ag_recv, fw_send, fw_recv, a_send, a_recv, b_send, b_recv, c_send, c_recv, out_sem,
):
    region = lax.axis_index("region")
    neuron = lax.axis_index("neuron")
    z, x_lo = region // 2, region % 2
    x_hi, y, core = neuron // 8, (neuron // 2) % 4, neuron % 2
    chip = neuron // 2
    x = x_hi * 2 + x_lo
    mate = (region, chip * 2 + 1 - core)

    plane = []
    for dx in range(4):
        for dy in range(4):
            if (dx, dy) != (0, 0):
                px, py = (x + dx) % 4, (y + dy) % 4
                plane.append(((z * 2 + px % 2), (px // 2) * 4 + py, px % 2))
    spread = []
    for dz in (0, 4, 3, 5, 2, 6, 1, 7):
        for dl in (1, 0):
            if (dz, dl) != (0, 0):
                spread.append((((z + dz) % 8), (x_lo + dl) % 2))

    barrier = pltpu.get_barrier_semaphore()
    for pz, lo in spread[1:]:
        pl.semaphore_signal(barrier, inc=1, device_id=(pz * 2 + lo, neuron), device_id_type=MESH)
    for reg, pos, _ in plane:
        pl.semaphore_signal(barrier, inc=1, device_id=(reg, pos * 2 + core), device_id_type=MESH)
    pl.semaphore_signal(barrier, inc=1, device_id=mate, device_id_type=MESH)

    own = []
    for h in range(2):
        copy = pltpu.make_async_copy(
            lat_hbm.at[:, pl.ds(h * LANES, LANES)], latb.at[core, h, chip], in_sem.at[h]
        )
        copy.start()
        own.append(copy)
    smalls = []
    for k, (source, target) in enumerate(((load_hbm, load_ref), (bias_hbm, bias_ref), (delay_hbm, delay_ref))):
        copy = pltpu.make_async_copy(source, target, in_sem.at[2 + k])
        copy.start()
        smalls.append(copy)
    block = NEU // ROWS
    loads = []
    for k in range(ROWS):
        rows = pl.ds(k * block, block)
        copy = pltpu.make_async_copy(counts_hbm.at[rows], counts.at[rows], cnt_sem.at[k])
        copy.start()
        loads.append(copy)

    for copy in smalls:
        copy.wait()
    ba, bb, bc = split_three(bias_ref[...])
    stacked = jnp.concatenate([load_ref[...].astype(F32), ba, bb, bc, jnp.zeros((DEPTH - LAT - 3, NEU), F32)], axis=0)
    load_t[...] = jnp.transpose(stacked).astype(BF16)
    tail = lax.broadcasted_iota(jnp.int32, (DEPTH - LAT, CHUNK), 0)
    for kind in range(4):
        piece[kind, LAT:] = jnp.where(tail < 3, 1.0, 0.0).astype(BF16)
    grad_load[...] = jnp.zeros_like(grad_load)
    bias_sum[...] = jnp.zeros_like(bias_sum)
    rot[0] = jnp.zeros((LAT, LANES), F32)
    spun[TILES] = jnp.zeros((LAT, LANES), F32)
    same = lax.broadcasted_iota(jnp.int32, (LAT, LAT), 0) == lax.broadcasted_iota(jnp.int32, (LAT, LAT), 1)
    delay = jnp.sum(jnp.where(same, delay_ref[...].astype(F32), 0.0), axis=1, keepdims=True).astype(jnp.int32)
    lane = lax.broadcasted_iota(jnp.int32, (LAT, LANES), 1)
    back = (lane - delay) & (LANES - 1)
    ahead = (lane + delay) & (LANES - 1)
    kept = lane >= delay
    near = lane + delay < LANES
    recorded = rec_ref[...].reshape(1, 1)
    for copy in own:
        copy.wait()
    pl.semaphore_wait(barrier, 1 + len(plane) + len(spread) - 1)
    sends = []

    def to_mate(h, pos):
        copy = pltpu.make_async_remote_copy(
            src_ref=latb.at[core, h, pos], dst_ref=latb.at[core, h, pos], send_sem=fw_send.at[h, pos],
            recv_sem=fw_recv.at[h, pos], device_id=mate, device_id_type=MESH,
        )
        copy.start()
        sends.append(copy)

    arrivals = []
    for h in (core, 1 - core):
        for dxh, dy in NEAR:
            px = 3 - x if dxh else x
            pos = (px // 2) * 4 + (y + dy) % 4
            copy = pltpu.make_async_remote_copy(
                src_ref=latb.at[core, h, chip], dst_ref=latb.at[core, h, chip], send_sem=ag_send.at[h, pos],
                recv_sem=ag_recv.at[h, chip], device_id=(z * 2 + px % 2, pos * 2 + core), device_id_type=MESH,
            )
            copy.start()
            sends.append(copy)
            if len(arrivals) < CHIPS - 1:
                arrivals.append(pos)
        to_mate(h, chip)

    def pass_on(h):
        for pos in arrivals:
            pltpu.make_async_copy(latb.at[core, h, chip], latb.at[core, h, pos], ag_recv.at[h, pos]).wait()
            to_mate(h, pos)

    def from_mate(h):
        for pos in [chip] + arrivals:
            pltpu.make_async_copy(latb.at[core, h, chip], latb.at[1 - core, h, pos], fw_recv.at[h, pos]).wait()

    def rotate(kind):
        for pos in range(CHIPS):
            source = latb[kind // 2, kind % 2, pos].astype(F32)
            rot[pos * 4 + kind + 1] = jnp.take_along_axis(source, back, axis=1)

    pass_on(core)
    from_mate(1 - core)
    rotate(0)
    rotate(3)
    for copy in loads:
        copy.wait()

    def chunk(kind, between):
        for pos in range(CHIPS):
            tile = pos * 4 + kind
            piece[kind, :LAT, pos * LANES : (pos + 1) * LANES] = jnp.where(kept, rot[tile + 1], rot[tile]).astype(BF16)
        bins = lax.broadcasted_iota(jnp.int32, (1, CHUNK), 1)
        bins = (bins // LANES) * (4 * LANES) + kind * LANES + bins % LANES
        live = bins < recorded
        shift = None
        for k in range(NEU // BLOCK):
            if k in between:
                between[k]()
            rows = slice(k * BLOCK, (k + 1) * BLOCK)
            eta = jnp.dot(load_t[rows], piece[kind], preferred_element_type=F32)
            observed = jnp.concatenate(
                [counts[rows, (pos * 4 + kind) * LANES : (pos * 4 + kind + 1) * LANES] for pos in range(CHIPS)], axis=1
            )
            resid = jnp.where(live, jnp.exp(eta) - observed.astype(F32), 0.0)
            total = resid[:, :LANES]
            for pos in range(1, CHIPS):
                total = total + resid[:, pos * LANES : (pos + 1) * LANES]
            bias_sum[rows] += total
            low = resid.astype(BF16)
            grad_load[:, rows] += lax.dot_general(
                piece[kind, :LAT], low, (((1,), (1,)), ((), ())), preferred_element_type=F32
            )
            part_shift = jnp.dot(load_ref[:, rows], low, preferred_element_type=F32)
            shift = part_shift if shift is None else shift + part_shift
        for pos in range(CHIPS):
            spun[pos * 4 + kind] = jnp.take_along_axis(shift[:, pos * LANES : (pos + 1) * LANES], ahead, axis=1)

    def advance(kind):
        for pos in range(CHIPS):
            tile = pos * 4 + kind
            moved = jnp.where(near, spun[tile], spun[tile + 1])
            part[kind, pos, 0] = moved[:HALF]
            part[kind, pos, 1] = moved[HALF:]

    def to_owner(kind):
        return pltpu.make_async_remote_copy(
            src_ref=part.at[kind], dst_ref=mate_in.at[kind % 2], send_sem=a_send.at[kind % 2],
            recv_sem=a_recv.at[kind % 2], device_id=mate, device_id_type=MESH,
        )

    me = chip * 2 + x_lo

    def reduce_plane(owner):
        for h in range(2):
            to_owner(2 * owner + h).wait_recv()
        largest = None
        for h in range(2):
            for pos in range(CHIPS):
                for lo in range(2):
                    total = part[2 * owner + h, pos, lo] + mate_in[h, pos, lo]
                    mate_in[h, pos, lo] = total
                    size = jnp.max(jnp.abs(total).reshape(HALF // 8, 8, LANES), axis=0)
                    largest = size if largest is None else jnp.maximum(largest, size)
        exponent = exponent_of(jnp.max(largest, axis=0, keepdims=True))
        for pos in range(CHIPS):
            for lo in range(2):
                for h in range(2):
                    pair[2 * pos + lo, h * HALF : (h + 1) * HALF] = encode(mate_in[h, pos, lo], exponent)
                pair[2 * pos + lo, LAT:] = stamp(exponent)
        for k, (reg, pos, lo) in enumerate(plane):
            pltpu.make_async_remote_copy(
                src_ref=pair.at[pos * 2 + lo], dst_ref=plane_in.at[me], send_sem=b_send.at[k],
                recv_sem=b_recv.at[me], device_id=(reg, pos * 2 + core), device_id_type=MESH,
            ).start()
        plane_in[me] = pair[me]

    def early():
        @pl.when(core == 1)
        def _():
            reduce_plane(1)

    chunk(0, {2: lambda: pass_on(1 - core)})
    from_mate(core)
    rotate(2)
    rotate(1)
    chunk(3, {})
    advance(3)

    @pl.when(core == 0)
    def _():
        to_owner(3).start()

    chunk(2, {})
    advance(2)

    @pl.when(core == 0)
    def _():
        to_owner(2).start()

    chunk(1, {3: early})
    advance(1)
    advance(0)

    @pl.when(core == 1)
    def _():
        to_owner(1).start()
        to_owner(0).start()

    write = [pltpu.make_async_copy(grad_load, out_load, out_sem.at[0])]
    write[0].start()

    @pl.when(core == 0)
    def _():
        reduce_plane(0)

    grad_bias[...] = jnp.sum(jnp.transpose(bias_sum[...]), axis=0, keepdims=True)
    write.append(pltpu.make_async_copy(grad_bias, out_bias, out_sem.at[1]))
    write[1].start()

    for _, pos, lo in plane:
        pltpu.make_async_copy(pair.at[0], plane_in.at[pos * 2 + lo], b_recv.at[pos * 2 + lo]).wait()
    total = decode(plane_in, 0)
    for k in range(1, 2 * CHIPS):
        total = total + decode(plane_in, k)
    exponent = exponent_of(jnp.max(jnp.abs(total), axis=0, keepdims=True))
    mine[:LAT] = encode(total, exponent)
    mine[LAT:] = stamp(exponent)
    for k, (pz, lo) in enumerate(spread):
        copy = pltpu.make_async_remote_copy(
            src_ref=mine, dst_ref=final_in.at[region], send_sem=c_send.at[k],
            recv_sem=c_recv.at[region], device_id=(pz * 2 + lo, neuron), device_id_type=MESH,
        )
        copy.start()
        sends.append(copy)
    final_in[region] = mine[...]
    for k in range(2):
        to_owner(k).wait_send()
    for k in range(len(plane)):
        pltpu.make_async_copy(pair.at[0], plane_in.at[0], b_send.at[k]).wait()
    for pz, lo in spread:
        pltpu.make_async_copy(mine, final_in.at[pz * 2 + lo], c_recv.at[pz * 2 + lo]).wait()
    for lo in range(2):
        total = decode(final_in, lo)
        for k in range(1, 8):
            total = total + decode(final_in, 2 * k + lo)
        for h in range(2):
            grad_lat[lo * HALF : (lo + 1) * HALF, h * LANES : (h + 1) * LANES] = total[h * HALF : (h + 1) * HALF]
    write.append(pltpu.make_async_copy(grad_lat, out_lat, out_sem.at[2]))
    write[2].start()
    for copy in write:
        copy.wait()
    for copy in sends:
        copy.wait_send()


def hand_over(lat_in, load_in, bias_in, lat_out, load_out, bias_out):
    lat_out[...] = lat_in[...]
    load_out[...] = load_in[...]
    bias_out[...] = bias_in[...]


def per_device(counts, latents, loadings, bias, delays, recorded):
    vmem = pl.BlockSpec(memory_space=pltpu.VMEM)
    anywhere = pl.BlockSpec(memory_space=pl.ANY)
    shapes = (
        jax.ShapeDtypeStruct((LAT, 2 * LANES), F32),
        jax.ShapeDtypeStruct((LAT, NEU), F32),
        jax.ShapeDtypeStruct((1, NEU), F32),
    )
    dma = pltpu.SemaphoreType.DMA
    results = pl.pallas_call(
        kernel,
        out_shape=shapes,
        in_specs=[anywhere] * 5 + [vmem],
        out_specs=(anywhere,) * 3,
        scratch_shapes=[
            pltpu.VMEM((NEU, TIME), BF16),
            pltpu.VMEM((LAT, NEU), BF16),
            pltpu.VMEM((1, NEU), F32),
            pltpu.VMEM((1, LAT), jnp.int32),
            pltpu.VMEM((2, 2, CHIPS, LAT, LANES), BF16),
            pltpu.VMEM((TILES + 1, LAT, LANES), F32),
            pltpu.VMEM((4, DEPTH, CHUNK), BF16),
            pltpu.VMEM((NEU, DEPTH), BF16),
            pltpu.VMEM((NEU, LANES), F32),
            pltpu.VMEM((TILES + 1, LAT, LANES), F32),
            pltpu.VMEM((4, CHIPS, 2, HALF, LANES), F32),
            pltpu.VMEM((2, CHIPS, 2, HALF, LANES), F32),
            pltpu.VMEM((2 * CHIPS, CODED, LANES), I16),
            pltpu.VMEM((2 * CHIPS, CODED, LANES), I16),
            pltpu.VMEM((CODED, LANES), I16),
            pltpu.VMEM((16, CODED, LANES), I16),
            pltpu.VMEM((LAT, 2 * LANES), F32),
            pltpu.VMEM((LAT, NEU), F32),
            pltpu.VMEM((1, NEU), F32),
            dma((5,)),
            dma((ROWS,)),
            dma((2, CHIPS)),
            dma((2, CHIPS)),
            dma((2, CHIPS)),
            dma((2, CHIPS)),
            dma((2,)),
            dma((2,)),
            dma((15,)),
            dma((16,)),
            dma((15,)),
            dma((16,)),
            dma((3,)),
        ],
        compiler_params=pltpu.CompilerParams(
            collective_id=0, has_side_effects=True, vmem_limit_bytes=58 * 2**20
        ),
    )(counts[0], latents, loadings[0], bias, delays, recorded)
    grad_lat, grad_load, grad_bias = pl.pallas_call(
        hand_over,
        out_shape=shapes,
        in_specs=[vmem] * 3,
        out_specs=(vmem,) * 3,
    )(*results)
    return grad_lat, grad_load[None], grad_bias


def solution(mesh):
    placed = (
        P("region", "neuron", None),
        P(None, "neuron"),
        P("region", None, "neuron"),
        P("region", "neuron"),
        P("region", None),
        P("region"),
    )
    return jax.shard_map(
        per_device,
        mesh=mesh,
        in_specs=placed,
        out_specs=(P(None, "neuron"), P("region", None, "neuron"), P("region", "neuron")),
        check_vma=False,
    )
```

time: 318 us -> 46.9 us (0.15)
  waiting for transfers between devices: 204 us -> 0 us
  Pallas kernels: 0 us -> 44.8 us
  matrix products: 35.2 us -> 0 us
  blocking collectives: 25.2 us -> 0 us
  local copies, waits for them, and re-layouts: 20.1 us -> 0 us
  other arithmetic: 16.5 us -> 0 us
  between operations: 14.2 us -> 1.29 us
    psum x1 -> x0, waiting for transfers between devices: 131 us -> none  [per_device(): grad_latents = lax.psum(summed, 'region')]
    reduce_scatter x1 -> x0, waiting for transfers between devices: 73.4 us -> none  [per_device(): summed = lax.psum_scatter(source, 'neuron', scatter_dimension=1, tiled=True)]
    pallas_call x0 -> x2, Pallas kernels: none -> 44.8 us  [the longest x1 43.1 us: per_device(): pl.pallas_call(kernel, out_shape=shapes, in_specs=[anywhere] * 5 + [vmem]...]
    dot_general x48 -> x0, matrix products: 35.2 us -> none  [the longest x16 26.2 us: accumulate(): lax.dot_general(load, piece, (((0,), (0,)), ((), ())), preferred_element_...]
    all_gather x1 -> x0, blocking collectives: 25.2 us -> none  [per_device(): whole = lax.all_gather(latents, 'neuron', axis=1, tiled=True)]
    unnamed x8 -> x0, local copies, waits for them, and re-layouts: 16.9 us -> none
    lt x16 -> x0, other arithmetic: 10.9 us -> none  [accumulate(): resid = jnp.where((bins < length)[None, :], jnp.exp(eta) - observed, 0.0)]
    select_n x16 -> x0, other arithmetic: 4.43 us -> none  [move_rows(): current = jnp.where(chosen[:, None], displaced, current)]
  transfers between devices with their start and end apart: 2 -> 0, of which waited for: 2 -> 0; matrix products, arithmetic and copies ran while one was open for 0% -> 0% of each run, Pallas kernels for 0% -> 0%
where the time goes in v2:
time: 46.9 us; the launch traced here: 46.1 us
  Pallas kernels  44.8 us (96%)
  between operations  1.29 us (3%)
    pallas_call x1, Pallas kernels, per_device(): pl.pallas_call(kernel, out_shape=shapes, in_specs=[anywhere] * 5 + [vmem]...  43.1 us
    pallas_call x1, Pallas kernels, per_device(): pl.pallas_call(hand_over, out_shape=shapes, in_specs=[vmem] * 3, out_spec...  1.74 us

profile of v2, /device:TPU:2, one launch (start us, length us, event | category | flops | bytes accessed | tf_op | source)
XLA Modules:
  0.0 46.1 jit_solution(14801859505723320517)
XLA Ops:
  1.3 43.1 %shard_map.85 = (f32[64,256]{1,0:T(8,128)}, f32[64,1280]{1,0:T(8,128)}, f32[1,1280]{1,0:T(1,128)}) custom-call(bf16[1280,4096]{1,0:T(8,128)(2,1)} %bitcast.3, bf16[64,256]{1,0:T(8,128)(2,1)} %lat_hbm.1, bf16[64,1280]{1,0:T(8,128)(2,1)} %bitcast.4, f32[1,1280]{1,0:T(1,128)} %bias_hbm.1, s32[1,64]{1,0:T(1,128)} %delay_hbm.1, s32[1]{0:T(128)S(6)} %copy.9.rec_ref), custom_call_target="tpu_custom_call" | custom-call | tf_op jit(solution)/shard_map/pallas_call | solution.py:340
  44.4 1.7 %shard_map.86 = (f32[64,256]{1,0:T(8,128)}, f32[64,1280]{1,0:T(8,128)}, f32[1,1280]{1,0:T(1,128)}) custom-call(f32[64,256]{1,0:T(8,128)} %get-tuple-element.9.lat_in, f32[64,1280]{1,0:T(8,128)} %get-tuple-element.10.load_in, f32[1,1280]{1,0:T(1,128)} %get-tuple-element.11.bias_in), custom_call_target="tpu_custom_call" | custom-call | tf_op jit(solution)/shard_map/pallas_call | solution.py:383

commit v3 on v2

--- a/solution.py
+++ b/solution.py
@@ -53,10 +53,10 @@
 
 def kernel(
     counts_hbm, lat_hbm, load_hbm, bias_hbm, delay_hbm, rec_ref,
-    out_lat, out_load, out_bias,
+    grad_lat, grad_load, grad_bias,
     counts, load_ref, bias_ref, delay_ref, latb, rot, piece, load_t, bias_sum, spun, part, mate_in, pair, plane_in,
-    mine, final_in, grad_lat, grad_load, grad_bias,
-    in_sem, cnt_sem, ag_send, ag_recv, fw_send, fw_recv, a_send, a_recv, b_send, b_recv, c_send, c_recv, out_sem,
+    mine, final_in,
+    in_sem, cnt_sem, ag_send, ag_recv, fw_send, fw_recv, a_send, a_recv, b_send, b_recv, c_send, c_recv,
 ):
     region = lax.axis_index("region")
     neuron = lax.axis_index("neuron")
@@ -104,6 +104,34 @@
         copy = pltpu.make_async_copy(counts_hbm.at[rows], counts.at[rows], cnt_sem.at[k])
         copy.start()
         loads.append(copy)
+
+    for copy in own:
+        copy.wait()
+    pl.semaphore_wait(barrier, 1 + len(plane) + len(spread) - 1)
+    sends = []
+
+    def to_mate(h, pos):
+        copy = pltpu.make_async_remote_copy(
+            src_ref=latb.at[core, h, pos], dst_ref=latb.at[core, h, pos], send_sem=fw_send.at[h, pos],
+            recv_sem=fw_recv.at[h, pos], device_id=mate, device_id_type=MESH,
+        )
+        copy.start()
+        sends.append(copy)
+
+    arrivals = []
+    for h in (core, 1 - core):
+        for dxh, dy in NEAR:
+            px = 3 - x if dxh else x
+            pos = (px // 2) * 4 + (y + dy) % 4
+            copy = pltpu.make_async_remote_copy(
+                src_ref=latb.at[core, h, chip], dst_ref=latb.at[core, h, chip], send_sem=ag_send.at[h, pos],
+                recv_sem=ag_recv.at[h, chip], device_id=(z * 2 + px % 2, pos * 2 + core), device_id_type=MESH,
+            )
+            copy.start()
+            sends.append(copy)
+            if len(arrivals) < CHIPS - 1:
+                arrivals.append(pos)
+        to_mate(h, chip)
 
     for copy in smalls:
         copy.wait()
@@ -125,33 +153,6 @@
     kept = lane >= delay
     near = lane + delay < LANES
     recorded = rec_ref[...].reshape(1, 1)
-    for copy in own:
-        copy.wait()
-    pl.semaphore_wait(barrier, 1 + len(plane) + len(spread) - 1)
-    sends = []
-
-    def to_mate(h, pos):
-        copy = pltpu.make_async_remote_copy(
-            src_ref=latb.at[core, h, pos], dst_ref=latb.at[core, h, pos], send_sem=fw_send.at[h, pos],
-            recv_sem=fw_recv.at[h, pos], device_id=mate, device_id_type=MESH,
-        )
-        copy.start()
-        sends.append(copy)
-
-    arrivals = []
-    for h in (core, 1 - core):
-        for dxh, dy in NEAR:
-            px = 3 - x if dxh else x
-            pos = (px // 2) * 4 + (y + dy) % 4
-            copy = pltpu.make_async_remote_copy(
-                src_ref=latb.at[core, h, chip], dst_ref=latb.at[core, h, chip], send_sem=ag_send.at[h, pos],
-                recv_sem=ag_recv.at[h, chip], device_id=(z * 2 + px % 2, pos * 2 + core), device_id_type=MESH,
-            )
-            copy.start()
-            sends.append(copy)
-            if len(arrivals) < CHIPS - 1:
-                arrivals.append(pos)
-        to_mate(h, chip)
 
     def pass_on(h):
         for pos in arrivals:
@@ -220,10 +221,9 @@
     me = chip * 2 + x_lo
 
     def reduce_plane(owner):
-        for h in range(2):
+        largest = None
+        for h in (1, 0):
             to_owner(2 * owner + h).wait_recv()
-        largest = None
-        for h in range(2):
             for pos in range(CHIPS):
                 for lo in range(2):
                     total = part[2 * owner + h, pos, lo] + mate_in[h, pos, lo]
@@ -268,23 +268,22 @@
 
     chunk(1, {3: early})
     advance(1)
+
+    @pl.when(core == 1)
+    def _():
+        to_owner(1).start()
+
     advance(0)
 
     @pl.when(core == 1)
     def _():
-        to_owner(1).start()
         to_owner(0).start()
 
-    write = [pltpu.make_async_copy(grad_load, out_load, out_sem.at[0])]
-    write[0].start()
-
     @pl.when(core == 0)
     def _():
         reduce_plane(0)
 
     grad_bias[...] = jnp.sum(jnp.transpose(bias_sum[...]), axis=0, keepdims=True)
-    write.append(pltpu.make_async_copy(grad_bias, out_bias, out_sem.at[1]))
-    write[1].start()
 
     for _, pos, lo in plane:
         pltpu.make_async_copy(pair.at[0], plane_in.at[pos * 2 + lo], b_recv.at[pos * 2 + lo]).wait()
@@ -314,10 +313,6 @@
             total = total + decode(final_in, 2 * k + lo)
         for h in range(2):
             grad_lat[lo * HALF : (lo + 1) * HALF, h * LANES : (h + 1) * LANES] = total[h * HALF : (h + 1) * HALF]
-    write.append(pltpu.make_async_copy(grad_lat, out_lat, out_sem.at[2]))
-    write[2].start()
-    for copy in write:
-        copy.wait()
     for copy in sends:
         copy.wait_send()
 
@@ -339,9 +334,9 @@
     dma = pltpu.SemaphoreType.DMA
     results = pl.pallas_call(
         kernel,
-        out_shape=shapes,
+        out_shape=tuple(pltpu.VMEM(part.shape, part.dtype) for part in shapes),
         in_specs=[anywhere] * 5 + [vmem],
-        out_specs=(anywhere,) * 3,
+        out_specs=(vmem,) * 3,
         scratch_shapes=[
             pltpu.VMEM((NEU, TIME), BF16),
             pltpu.VMEM((LAT, NEU), BF16),
@@ -359,9 +354,6 @@
             pltpu.VMEM((2 * CHIPS, CODED, LANES), I16),
             pltpu.VMEM((CODED, LANES), I16),
             pltpu.VMEM((16, CODED, LANES), I16),
-            pltpu.VMEM((LAT, 2 * LANES), F32),
-            pltpu.VMEM((LAT, NEU), F32),
-            pltpu.VMEM((1, NEU), F32),
             dma((5,)),
             dma((ROWS,)),
             dma((2, CHIPS)),
@@ -374,7 +366,6 @@
             dma((16,)),
             dma((15,)),
             dma((16,)),
-            dma((3,)),
         ],
         compiler_params=pltpu.CompilerParams(
             collective_id=0, has_side_effects=True, vmem_limit_bytes=58 * 2**20
@@ -385,7 +376,7 @@
         out_shape=shapes,
         in_specs=[vmem] * 3,
         out_specs=(vmem,) * 3,
-    )(*results)
+    )(*[pltpu.with_memory_space_constraint(part, pltpu.VMEM) for part in results])
     return grad_lat, grad_load[None], grad_bias
 
 

time: 46.9 us -> 44.4 us (0.947); the launches traced: 46.1 us -> 44.3 us
  Pallas kernels: 44.8 us -> 43 us
    pallas_call x1, Pallas kernels: 1.74 us -> 0.77 us  [per_device(): pl.pallas_call(hand_over, out_shape=shapes, in_specs=[vmem] * 3, out_spec...]
    pallas_call x1, Pallas kernels: 43.1 us -> 42.2 us  [per_device(): pl.pallas_call(kernel, out_shape=tuple((pltpu.VMEM(part.shape, part.dtype...]
where the time goes in v3:
time: 44.4 us; the launch traced here: 44.3 us
  Pallas kernels  43 us (97%)
  between operations  1.29 us (3%)
    pallas_call x1, Pallas kernels, per_device(): pl.pallas_call(kernel, out_shape=tuple((pltpu.VMEM(part.shape, part.dtype...  42.2 us

profile of v3, /device:TPU:2, one launch (start us, length us, event | category | flops | bytes accessed | tf_op | source)
XLA Modules:
  0.0 44.3 jit_solution(18434426935078074026)
XLA Ops:
  1.3 42.2 %shard_map.85 = (f32[64,256]{1,0:T(8,128)S(1)}, f32[64,1280]{1,0:T(8,128)S(1)}, f32[1,1280]{1,0:T(1,128)S(1)}) custom-call(bf16[1280,4096]{1,0:T(8,128)(2,1)} %bitcast.3, bf16[64,256]{1,0:T(8,128)(2,1)} %lat_hbm.1, bf16[64,1280]{1,0:T(8,128)(2,1)} %bitcast.4, f32[1,1280]{1,0:T(1,128)} %bias_hbm.1, s32[1,64]{1,0:T(1,128)} %delay_hbm.1, s32[1]{0:T(128)S(6)} %copy.9.rec_ref), custom_call_target="tpu_custom_call" | custom-call | tf_op jit(solution)/shard_map/pallas_call | solution.py:335
  43.5 0.8 %shard_map.86 = (f32[64,256]{1,0:T(8,128)}, f32[64,1280]{1,0:T(8,128)}, f32[1,1280]{1,0:T(1,128)}) custom-call(f32[64,256]{1,0:T(8,128)S(1)} %get-tuple-element.9.lat_in, f32[64,1280]{1,0:T(8,128)S(1)} %get-tuple-element.10.load_in, f32[1,1280]{1,0:T(1,128)S(1)} %get-tuple-element.11.bias_in), custom_call_target="tpu_custom_call" | custom-call | tf_op jit(solution)/shard_map/pallas_call | solution.py:374
